TPU v7x, 32 devices: a whole 2x2x4 slice. The times are simulated.
32 devices in a mesh: groups: 2 (over x), rows: 16 (over z, y, core).
Axes of the slice: x: 2, y: 2, z: 4, core: 2. Of those that a mesh axis runs over, the one named last changes fastest.
Arguments:
- genotypes: bfloat16 [32768, 4096], P(('groups', 'rows')), parts along dimension 0, may hold values from -6 to 6
- sample_factors: float32 [32768, 64], P(('groups', 'rows')), parts along dimension 0, may hold values from -2.1213203 to 2.1213203
- snp_factors: float32 [20480, 64], P(('groups', 'rows')), parts along dimension 0, may hold values from -2.1213203 to 2.1213203
- coverage: int32 [32, 64], P('groups'), parts along dimension 0, may hold values from 0 to 159, as said below
Outputs:
- new_samples: float32 [32768, 64], P(('groups', 'rows')), parts along dimension 0
- new_snps: float32 [20480, 64], P(('groups', 'rows')), parts along dimension 0
There are 2 independent parts, one for each index of `groups`. A program takes and returns all parts, laid end to end along the dimension named above; each array names one. Nothing has to cross between parts.
Inputs may be any that keep to these rules, and one draw needn't show every extreme that they name: `coverage`: each row lists 64 distinct SNP blocks in ascending order, exactly 4 of them among blocks o * 10 to (o + 1) * 10 - 1 for every o; every SNP block is listed by at least one batch.
All inputs are finite; a program needn't handle non-finite values.
Results may differ from a plain program's by a relative error of at most 0.0067.
Values may be sent and summed in bfloat16 or wider, within the bound.
A program may use at most 128 MiB of HBM per device.

v0:
```python
import math

import jax
import jax.numpy as jnp
from jax import lax
from jax.sharding import PartitionSpec as P

ROUNDS = 2


weight_decay = 0.02


def on_device(genotypes, sample_factors, snp_factors, coverage):
    devices = lax.axis_size("rows")
    position = lax.axis_index("rows")
    samples_here = genotypes.shape[0]
    rank_width = sample_factors.shape[1]
    covered = coverage.shape[1]
    tile_size = genotypes.shape[1] // covered
    per_owner = covered // devices
    own_blocks = snp_factors.shape[0] // tile_size
    own_list = lax.dynamic_index_in_dim(coverage, position, 0, keepdims=False)
    local_list = (
        lax.dynamic_slice_in_dim(coverage, position * per_owner, per_owner, 1)
        - position * own_blocks
    )
    one_hot = (
        local_list[:, :, None] == jnp.arange(own_blocks, dtype=jnp.int32)[None, None, :]
    ).astype(jnp.float32)
    observers = jnp.sum(one_hot, axis=(0, 1))
    snp_step = 0.5 * math.sqrt(rank_width) / (samples_here * observers)
    sample_step = 0.5 * math.sqrt(rank_width) / (covered * tile_size)
    samples = sample_factors
    snps = snp_factors
    for iteration in range(ROUNDS):
        snp_bf16 = snps.astype(jnp.bfloat16).reshape(own_blocks, tile_size, rank_width)
        gathered = lax.all_gather(snp_bf16, "rows", axis=0, tiled=True)
        panels = gathered[own_list].reshape(covered * tile_size, rank_width)
        predicted = lax.dot_general(
            samples.astype(jnp.bfloat16),
            panels,
            (((1,), (1,)), ((), ())),
            preferred_element_type=jnp.float32,
        )
        residual = (genotypes.astype(jnp.float32) - predicted).astype(jnp.bfloat16)
        gradient = jnp.dot(residual, panels, preferred_element_type=jnp.float32)
        samples = (1.0 - weight_decay) * samples + sample_step * gradient
        sample_bf16 = samples.astype(jnp.bfloat16)
        predicted = lax.dot_general(
            sample_bf16, panels, (((1,), (1,)), ((), ())), preferred_element_type=jnp.float32
        )
        residual = (genotypes.astype(jnp.float32) - predicted).astype(jnp.bfloat16)
        snp_gradient = lax.dot_general(
            residual, sample_bf16, (((0,), (0,)), ((), ())), preferred_element_type=jnp.float32
        )
        incoming_terms = lax.all_to_all(
            snp_gradient.reshape(devices, per_owner, tile_size, rank_width).astype(jnp.bfloat16),
            "rows",
            split_axis=0,
            concat_axis=0,
            tiled=True,
        ).astype(jnp.float32)
        summed = jnp.einsum(
            "bpk,bptr->ktr", one_hot, incoming_terms, precision=lax.Precision.HIGHEST
        )
        snps = (1.0 - weight_decay) * snps + (snp_step[:, None, None] * summed).reshape(
            own_blocks * tile_size, rank_width
        )
    return (samples, snps)


def solution(mesh):
    placed = (
        P(("groups", "rows"), None),
        P(("groups", "rows"), None),
        P(("groups", "rows"), None),
        P("groups", None),
    )
    return jax.shard_map(
        on_device,
        mesh=mesh,
        in_specs=placed,
        out_specs=(P(("groups", "rows"), None), P(("groups", "rows"), None)),
        check_vma=False,
    )
```

profile of v0, /device:TPU:0, one launch (start us, length us, event | category | flops | bytes accessed | tf_op | source)
XLA Modules:
  0.0 190.6 jit_solution(12273409029608411657)
XLA Ops:
  7.2 0.0 all-gather.3.cloned.1.call-start
  7.2 1.1 copy.32
  8.3 0.7 convert_element_type.52
  9.0 0.0 all-gather.3.cloned.1.call-update
  9.0 0.0 copy-start
  9.0 0.0 copy-start.1
  9.0 12.1 %copy.31 = bf16[1024,4096]{0,1:T(8,128)(2,1)} copy(bf16[1024,4096]{1,0:T(8,128)(2,1)} %param.4) | data formatting | bytes 16777216 | tf_op args[0]
  21.1 0.0 copy-done
  21.1 35.6 %all-gather.3.cloned.1.call-done = bf16[160,64,64]{2,1,0:T(8,128)(2,1)} async-done(((bf16[10,64,64]{2,1,0:T(8,128)(2,1)}), bf16[160,64,64]{2,1,0:T(8,128)(2,1)}) %all-gather.3.cloned.1.call-update) | async-done | bytes 1310736 | tf_op jit(solution)/shard_map/all_gather | solution.py:38
  56.8 2.5 %gather_fusion = bf16[64,64,64]{2,1,0:T(8,128)(2,1)S(1)} fusion(bf16[160,64,64]{2,1,0:T(8,128)(2,1)} %all-gather.3.cloned.1.call-done, s32[1024]{0:T(1024)S(1)} %pad_clamp_fusion), kind=kCustom, calls=%fused_computation | custom fusion | bytes 1048832 | tf_op jit(solution)/shard_map/gather | solution.py:39
  59.3 0.0 copy-done.1
  59.3 7.2 %fusion.11 = f32[1024,64]{0,1:T(8,128)S(1)} fusion(bf16[4096,64]{1,0:T(8,128)(2,1)S(1)} %bitcast.58, bf16[1024,4096]{0,1:T(8,128)(2,1)} %copy.31, f32[1024,64]{0,1:T(8,128)S(1)} %copy-done.1), kind=kOutput, calls=%fused_computation.21 | convolution fusion | flops 1086586880 | bytes 9437184 | tf_op jit(solution)/shard_map/dot_general | solution.py:47
  66.5 8.1 %convolution_convert_fusion.1 = bf16[4096,64]{0,1:T(8,128)(2,1)S(1)} fusion(bf16[1024,4096]{0,1:T(8,128)(2,1)} %copy.31, bf16[4096,64]{1,0:T(8,128)(2,1)S(1)} %bitcast.59, f32[1024,64]{0,1:T(8,128)S(1)} %fusion.11), kind=kOutput, calls=%fused_computation.11 | convolution fusion | flops 1086717952 | bytes 9699328 | tf_op jit(solution)/shard_map/dot_general | solution.py:54
  74.6 1.1 convert_element_type.59
  75.7 1.9 copy.36
  77.6 1.5 reshape.84
  79.2 3.6 %all-to-all-start = ((bf16[16,2,8192]{2,1,0:T(2,128)(2,1)}), bf16[16,2,8192]{2,1,0:T(2,128)(2,1)S(1)}, u32[]{:S(2)}, u32[]{:S(2)}) async-start(bf16[16,2,8192]{2,1,0:T(2,128)(2,1)} %reshape.84), calls=%async_computation | async-start | bytes 1048576 | tf_op jit(solution)/shard_map/all_to_all | solution.py:57
  82.8 0.2 all-gather.5.cloned.1.call-start
  83.0 0.1 constant_dynamic-slice_fusion
  83.1 0.1 copy.50
  83.2 0.1 convert_reduce_fusion
  83.3 13.9 %all-to-all-done = bf16[16,2,8192]{2,1,0:T(2,128)(2,1)S(1)} async-done(((bf16[16,2,8192]{2,1,0:T(2,128)(2,1)}), bf16[16,2,8192]{2,1,0:T(2,128)(2,1)S(1)}, u32[]{:S(2)}, u32[]{:S(2)}) %all-to-all-start) | async-done | bytes 524320 | tf_op jit(solution)/shard_map/all_to_all | solution.py:57
  97.2 0.7 reshape.85
  97.9 0.7 fusion.7
  98.6 0.1 copy.38
  98.7 0.7 fusion.18
  99.4 0.0 all-gather.5.cloned.1.call-update
  99.4 42.7 %all-gather.5.cloned.1.call-done = bf16[160,64,64]{2,1,0:T(8,128)(2,1)} async-done(((bf16[10,64,64]{2,1,0:T(8,128)(2,1)}), bf16[160,64,64]{2,1,0:T(8,128)(2,1)}) %all-gather.5.cloned.1.call-update) | async-done | bytes 1310736 | tf_op jit(solution)/shard_map/all_gather | solution.py:38
  142.1 2.5 %gather_fusion.1 = bf16[64,64,64]{2,1,0:T(8,128)(2,1)S(1)} fusion(bf16[160,64,64]{2,1,0:T(8,128)(2,1)} %all-gather.5.cloned.1.call-done, s32[1024]{0:T(1024)S(1)} %pad_clamp_fusion), kind=kCustom, calls=%fused_computation.1 | custom fusion | bytes 1048832 | tf_op jit(solution)/shard_map/gather | solution.py:39
  144.6 7.1 %fusion.10 = f32[1024,64]{0,1:T(8,128)S(1)} fusion(bf16[4096,64]{1,0:T(8,128)(2,1)S(1)} %bitcast.56, bf16[1024,4096]{0,1:T(8,128)(2,1)} %copy.31, f32[1024,64]{0,1:T(8,128)S(1)} %fusion.11), kind=kOutput, calls=%fused_computation.20 | convolution fusion | flops 1086586880 | bytes 9437184 | tf_op jit(solution)/shard_map/dot_general | solution.py:47
  151.7 0.0 copy-start.2
  151.7 8.2 %convolution_convert_fusion = bf16[4096,64]{0,1:T(8,128)(2,1)S(1)} fusion(bf16[1024,4096]{0,1:T(8,128)(2,1)} %copy.31, bf16[4096,64]{1,0:T(8,128)(2,1)S(1)} %bitcast.57, f32[1024,64]{0,1:T(8,128)S(1)} %fusion.10), kind=kOutput, calls=%fused_computation.10 | convolution fusion | flops 1086717952 | bytes 9699328 | tf_op jit(solution)/shard_map/dot_general | solution.py:54
  160.0 1.1 convert_element_type.65
  161.1 1.9 copy.41
  163.0 0.7 reshape.86
  163.7 0.0 copy-done.2
  163.7 17.6 %all_to_all.10 = bf16[16,2,8192]{2,1,0:T(2,128)(2,1)S(1)} all-to-all(bf16[16,2,8192]{2,1,0:T(2,128)(2,1)S(1)} %reshape.86), channel_id=1, replica_groups=mesh['groups'=2,'rows'=16] {'rows'}, dimensions={0} | all-to-all | bytes 1048576 | tf_op jit(solution)/shard_map/all_to_all | solution.py:57
  181.4 0.7 reshape.87
  182.0 0.7 fusion.6
  182.7 0.1 copy.43
  182.8 0.1 bitcast_add_fusion
  182.9 0.8 copy.44
  (4 shorter events, 0.0 us)
Async XLA Ops:
  7.2 49.6 %all-gather.3.cloned.1.call-start = ((), (), s32[]{:S(2)}) async-start(), calls=%async_computation.2 | async-start | bytes 2785280 | tf_op jit(solution)/shard_map/all_gather | solution.py:38
  9.0 12.1 %copy-start = (s32[16,64]{1,0:T(8,128)S(1)}, s32[16,64]{1,0:T(8,128)}, u32[]{:S(2)}) copy-start(s32[16,64]{1,0:T(8,128)} %param.7) | copy-start | bytes 12292
  9.0 50.3 %copy-start.1 = (f32[1024,64]{0,1:T(8,128)S(1)}, f32[1024,64]{0,1:T(8,128)}, u32[]{:S(2)}) copy-start(f32[1024,64]{0,1:T(8,128)} %param.5) | copy-start | bytes 786436
  79.2 18.0 %all-to-all-start = ((bf16[16,2,8192]{2,1,0:T(2,128)(2,1)}), bf16[16,2,8192]{2,1,0:T(2,128)(2,1)S(1)}, u32[]{:S(2)}, u32[]{:S(2)}) async-start(bf16[16,2,8192]{2,1,0:T(2,128)(2,1)} %reshape.84), calls=%async_computation | async-start | bytes 1048576 | tf_op jit(solution)/shard_map/all_to_all | solution.py:57
  82.8 59.3 %all-gather.5.cloned.1.call-start = ((), (), s32[]{:S(2)}) async-start(), calls=%async_computation.3 | async-start | bytes 2785280 | tf_op jit(solution)/shard_map/all_gather | solution.py:38
  151.7 12.0 %copy-start.2 = (f32[1024,64]{0,1:T(8,128)}, f32[1024,64]{0,1:T(8,128)S(1)}, u32[]{:S(2)}) copy-start(f32[1024,64]{0,1:T(8,128)S(1)} %fusion.10) | copy-start | bytes 786436
Sparse Core Ops, SparseCore 0:
  10.9 45.8 all-gather.2
  99.5 42.4 all-gather.4
where the time goes:
time: 191 us
  waiting for transfers between devices  92.2 us (48%)
  matrix products  32.1 us (17%)
  local copies, waits for them, and re-layouts  29 us (15%)
  blocking collectives  17.6 us (9%)
  between operations  14.2 us (7%)
  starting transfers between devices  3.83 us (2%)
    all_gather x2, waiting for transfers between devices, on_device(): gathered = lax.all_gather(snp_bf16, 'rows', axis=0, tiled=True)  78.3 us
    unnamed x14, local copies, waits for them, and re-layouts  17.6 us
    all_to_all x1, blocking collectives, on_device(): lax.all_to_all(snp_gradient.reshape(devices, per_owner, tile_size, rank_w...  17.6 us
    dot_general x2, matrix products, on_device(): lax.dot_general(residual, sample_bf16, (((0,), (0,)), ((), ())), preferre...  16.4 us
    dot_general x2, matrix products, on_device(): gradient = jnp.dot(residual, panels, preferred_element_type=jnp.float32)  14.3 us
    all_to_all x1, waiting for transfers between devices, on_device(): lax.all_to_all(snp_gradient.reshape(devices, per_owner, tile_size, rank_w...  13.9 us
    convert_element_type x4, local copies, waits for them, and re-layouts, on_device(): snp_gradient.reshape(devices, per_owner, tile_size, rank_width)  6.07 us
    gather x2, local copies, waits for them, and re-layouts, on_device(): panels = gathered[own_list].reshape(covered * tile_size, rank_width)  4.97 us
  transfers between devices with their start and end apart: 3, of which 3 were waited for; matrix products, arithmetic and copies ran while one was open for 7% of the time, Pallas kernels for 0%

commit v1 on v0

v1 whole, which is shorter than its diff:
```python
import functools
import math

import jax
import jax.numpy as jnp
from jax import lax
from jax.experimental import pallas as pl
from jax.experimental.pallas import tpu as pltpu
from jax.sharding import PartitionSpec as P

ROUNDS = 2
DECAY = 0.02
MESH = pl.DeviceIdType.MESH
F32 = jnp.float32
BF16 = jnp.bfloat16


def nt(a, b):
    return lax.dot_general(a, b, (((1,), (1,)), ((), ())), preferred_element_type=F32)


def nn(a, b):
    return lax.dot_general(a, b, (((1,), (0,)), ((), ())), preferred_element_type=F32)


def three_terms(a):
    hi = a.astype(BF16)
    rest = a - hi.astype(F32)
    mid = rest.astype(BF16)
    low = (rest - mid.astype(F32)).astype(BF16)
    return hi, mid, low


def kernel(n, per, own, tile, cov_ref, geno_hbm, st_in, vt_in, st_out, vt_out,
           geno, panels, stage, terms, outgoing, blocks, st, st_bf, acc, total, count,
           geno_sem, send_sem, recv_sem):
    me = lax.axis_index("rows")
    width = per * tile
    rank = st.shape[0]
    rows = st.shape[1]

    def peer(d):
        return lax.rem(me + d, n)

    def source(d):
        return lax.rem(me - d + n, n)

    def geno_copy(c):
        return pltpu.make_async_copy(
            geno_hbm.at[:, pl.ds(pl.multiple_of(c * width, width), width)],
            geno.at[c], geno_sem.at[c])

    def push(phase, src, dst, there, slot):
        return pltpu.make_async_remote_copy(
            src_ref=src, dst_ref=dst, send_sem=send_sem.at[phase, there],
            recv_sem=recv_sem.at[phase, slot],
            device_id={"rows": there}, device_id_type=MESH)

    def panel_push(r, there, slot):
        return push(2 * r, stage.at[r, there], panels.at[r, slot], there, slot)

    def term_push(r, there, slot):
        return push(2 * r + 1, outgoing.at[r, there], terms.at[r, slot], there, slot)

    barrier = pltpu.get_barrier_semaphore()

    @pl.loop(1, n)
    def _(d):
        pl.semaphore_signal(barrier, inc=1, device_id={"rows": peer(d)}, device_id_type=MESH)

    @pl.loop(0, n)
    def _(d):
        geno_copy(source(d)).start()

    st[...] = st_in[...]
    for c in range(own):
        blocks[c] = vt_in[:, c * tile:(c + 1) * tile]

    def local(b, k):
        return jnp.clip(cov_ref[b, me * per + k] - me * own, 0, own - 1)

    def select(b):
        return jnp.concatenate([blocks[local(b, k)] for k in range(per)], axis=1).astype(BF16)

    place = lax.broadcasted_iota(jnp.int32, (1, width), 1) // tile

    def listed(b):
        out = jnp.full((1, width), local(b, 0), jnp.int32)
        for k in range(1, per):
            out = jnp.where(place == k, local(b, k), out)
        return out

    @pl.loop(0, n)
    def _(b):
        stage[0, b] = select(b)

    pl.semaphore_wait(barrier, n - 1)

    step = 0.5 * math.sqrt(rank) / (n * per * tile)
    for r in range(ROUNDS):
        if r > 0:
            @pl.loop(0, n)
            def _(b):
                stage[r, b] = select(b)

        @pl.loop(1, n)
        def _(d):
            panel_push(r, peer(d), me).start()

        panels[r, me] = stage[r, me]

        if r == 0:
            count[...] = jnp.zeros_like(count)

            @pl.loop(0, n)
            def _(b):
                row = listed(b)
                for c in range(own):
                    count[c:c + 1, :] += (row == c).astype(F32)

        st_bf[...] = st[...].astype(BF16)

        def sample_terms(s, square):
            panel = panels[r, s]
            acc[...] += nt(geno[s], panel)
            return square + nt(panel, panel)

        acc[...] = jnp.zeros_like(acc)
        if r == 0:
            geno_copy(me).wait()
        square = sample_terms(me, jnp.zeros((rank, rank), F32))

        def sample_body(d, square):
            s = source(d)
            panel_push(r, s, s).wait_recv()
            if r == 0:
                geno_copy(s).wait()
            return sample_terms(s, square)

        square = lax.fori_loop(1, n, sample_body, square)
        now = st_bf[...]
        fit = sum(nn(part, now) for part in three_terms(square))
        fresh = (1.0 - DECAY) * st[...] + step * (acc[...].T - fit)
        st[...] = fresh
        now = fresh.astype(BF16)
        st_bf[...] = now

        gram = three_terms(nt(now, now))

        def snp_term(s):
            panel = panels[r, s]
            fit = sum(nn(part, panel) for part in gram)
            return (nn(st_bf[...], geno[s]) - fit).astype(BF16)

        @pl.loop(1, n)
        def _(d):
            s = peer(d)
            outgoing[r, s] = snp_term(s)
            term_push(r, s, me).start()

        def add_term(b, value):
            row = listed(b)
            wide = value.astype(F32)
            for c in range(own):
                total[c] += jnp.where(row == c, wide, 0.0)

        total[...] = jnp.zeros_like(total)
        add_term(me, snp_term(me))

        @pl.loop(1, n)
        def _(d):
            b = source(d)
            term_push(r, b, b).wait_recv()
            add_term(b, terms[r, b])

        for c in range(own):
            observed = jnp.sum(count[c:c + 1, :], axis=1, keepdims=True) / tile
            rate = 0.5 * math.sqrt(rank) / (rows * observed)
            summed = total[c]
            gradient = sum(summed[:, k * tile:(k + 1) * tile] for k in range(per))
            blocks[c] = (1.0 - DECAY) * blocks[c] + rate * gradient

    st_out[...] = st[...]
    vt_out[...] = jnp.concatenate([blocks[c] for c in range(own)], axis=1)

    @pl.loop(1, n)
    def _(d):
        s = peer(d)
        for r in range(ROUNDS):
            panel_push(r, s, s).wait_send()
            term_push(r, s, s).wait_send()


def on_device(genotypes, sample_factors, snp_factors, coverage):
    n = lax.axis_size("rows")
    rows, rank = sample_factors.shape
    covered = coverage.shape[1]
    tile = genotypes.shape[1] // covered
    per = covered // n
    own = snp_factors.shape[0] // tile
    width = per * tile
    st, vt = pl.pallas_call(
        functools.partial(kernel, n, per, own, tile),
        out_shape=(
            jax.ShapeDtypeStruct((rank, rows), F32),
            jax.ShapeDtypeStruct((rank, own * tile), F32),
        ),
        in_specs=[
            pl.BlockSpec(memory_space=pltpu.SMEM),
            pl.BlockSpec(memory_space=pl.ANY),
            pl.BlockSpec(memory_space=pltpu.VMEM),
            pl.BlockSpec(memory_space=pltpu.VMEM),
        ],
        out_specs=(
            pl.BlockSpec(memory_space=pltpu.VMEM),
            pl.BlockSpec(memory_space=pltpu.VMEM),
        ),
        scratch_shapes=[
            pltpu.VMEM((n, rows, width), BF16),
            pltpu.VMEM((ROUNDS, n, rank, width), BF16),
            pltpu.VMEM((ROUNDS, n, rank, width), BF16),
            pltpu.VMEM((ROUNDS, n, rank, width), BF16),
            pltpu.VMEM((ROUNDS, n, rank, width), BF16),
            pltpu.VMEM((own, rank, tile), F32),
            pltpu.VMEM((rank, rows), F32),
            pltpu.VMEM((rank, rows), BF16),
            pltpu.VMEM((rows, rank), F32),
            pltpu.VMEM((own, rank, width), F32),
            pltpu.VMEM((own, width), F32),
            pltpu.SemaphoreType.DMA((n,)),
            pltpu.SemaphoreType.DMA((2 * ROUNDS, n)),
            pltpu.SemaphoreType.DMA((2 * ROUNDS, n)),
        ],
        compiler_params=pltpu.CompilerParams(
            collective_id=0, has_side_effects=True, vmem_limit_bytes=52 * 1024 * 1024
        ),
    )(coverage, genotypes, sample_factors.T, snp_factors.T)
    return st.T, vt.T


def solution(mesh):
    placed = P(("groups", "rows"), None)
    return jax.shard_map(
        on_device,
        mesh=mesh,
        in_specs=(placed, placed, placed, P("groups", None)),
        out_specs=(placed, placed),
        check_vma=False,
    )
```

time: 191 us -> 68.6 us (0.36)
  the two profiles are of different devices: /device:TPU:0 before, /device:TPU:13 now
where the time goes in v1:
time: 68.6 us; the launch traced here: 68.4 us
  Pallas kernels  63.8 us (93%)
  local copies, waits for them, and re-layouts  3.93 us (6%)
    pallas_call x1, Pallas kernels, on_device(): pl.pallas_call(functools.partial(kernel, n, per, own, tile), out_shape=(j...  63.8 us
    unnamed x8, local copies, waits for them, and re-layouts  3.93 us

profile of v1, /device:TPU:13, one launch (start us, length us, event | category | flops | bytes accessed | tf_op | source)
XLA Modules:
  0.0 68.4 jit_solution(9066431694618892355)
XLA Ops:
  0.6 0.0 copy-start
  0.6 0.9 %copy-done = f32[1024,64]{0,1:T(8,128)S(1)} copy-done((f32[1024,64]{0,1:T(8,128)S(1)}, f32[1024,64]{0,1:T(8,128)}, u32[]{:S(2)}) %copy-start) | copy-done | bytes 262168
  1.6 0.0 copy-start.1
  1.6 0.9 %copy-done.1 = f32[640,64]{0,1:T(8,128)S(1)} copy-done((f32[640,64]{0,1:T(8,128)S(1)}, f32[640,64]{0,1:T(8,128)}, u32[]{:S(2)}) %copy-start.1) | copy-done | bytes 163864
  2.5 0.0 copy-start.2
  2.5 0.7 %copy-done.2 = s32[16,64]{1,0:T(8,128)S(1)} copy-done((s32[16,64]{1,0:T(8,128)S(1)}, s32[16,64]{1,0:T(8,128)}, u32[]{:S(2)}) %copy-start.2) | copy-done | bytes 4120
  3.2 63.8 %shard_map.59 = (f32[64,1024]{1,0:T(8,128)S(1)}, f32[64,640]{1,0:T(8,128)S(1)}) custom-call(s32[16,64]{1,0:T(8,128)S(1)} %copy-done.2, bf16[1024,4096]{1,0:T(8,128)(2,1)} %geno_hbm.1, f32[64,1024]{1,0:T(8,128)S(1)} %bitcast.4, f32[64,640]{1,0:T(8,128)S(1)} %bitcast.7), custom_call_target="tpu_custom_call" | custom-call | tf_op jit(solution)/shard_map/pallas_call | solution.py:202
  67.0 0.7 %copy.8 = f32[1024,64]{0,1:T(8,128)} copy(f32[1024,64]{0,1:T(8,128)S(1)} %bitcast.5) | data formatting | bytes 524288
  67.7 0.7 copy.9
Async XLA Ops:
  0.6 1.0 %copy-start = (f32[1024,64]{0,1:T(8,128)S(1)}, f32[1024,64]{0,1:T(8,128)}, u32[]{:S(2)}) copy-start(f32[1024,64]{0,1:T(8,128)} %param.5) | copy-start | bytes 786436
  1.6 0.9 %copy-start.1 = (f32[640,64]{0,1:T(8,128)S(1)}, f32[640,64]{0,1:T(8,128)}, u32[]{:S(2)}) copy-start(f32[640,64]{0,1:T(8,128)} %param.6) | copy-start | bytes 491524
  2.5 0.7 %copy-start.2 = (s32[16,64]{1,0:T(8,128)S(1)}, s32[16,64]{1,0:T(8,128)}, u32[]{:S(2)}) copy-start(s32[16,64]{1,0:T(8,128)} %cov_ref.1) | copy-start | bytes 12292

commit v2 on v1

v2 whole, which is shorter than its diff:
```python
import functools
import math

import jax
import jax.numpy as jnp
from jax import lax
from jax.experimental import pallas as pl
from jax.experimental.pallas import tpu as pltpu
from jax.sharding import PartitionSpec as P

ROUNDS = 2
DECAY = 0.02
MESH = pl.DeviceIdType.MESH
F32 = jnp.float32
BF16 = jnp.bfloat16


def nt(a, b):
    return lax.dot_general(a, b, (((1,), (1,)), ((), ())), preferred_element_type=F32)


def nn(a, b):
    return lax.dot_general(a, b, (((1,), (0,)), ((), ())), preferred_element_type=F32)


def three_terms(a):
    hi = a.astype(BF16)
    rest = a - hi.astype(F32)
    mid = rest.astype(BF16)
    low = (rest - mid.astype(F32)).astype(BF16)
    return hi, mid, low


def kernel(n, group, per, own, tile, cov_ref, geno_hbm, st_in, vt_in, st_out, vt_out,
           geno, panels, stage, terms, outgoing, whole, part_out, part_in, pairs, seen, grads,
           st, st_bf, acc, total, count,
           geno_sem, panel_send, panel_recv, term_send, term_recv,
           whole_send, whole_recv, part_send, part_recv):
    me = lax.axis_index("rows")
    levels = n // group
    z, i = lax.div(me, group), lax.rem(me, group)
    width = per * tile
    two = 2 * tile
    rank = st.shape[0]
    rows = st.shape[1]

    def at(level, place):
        return level * group + place

    def mate(j):
        return lax.rem(i + j, group)

    def after(d):
        return lax.rem(z + d, levels)

    def before(d):
        return lax.rem(z - d + levels, levels)

    def geno_copy(c):
        return pltpu.make_async_copy(
            geno_hbm.at[:, pl.ds(pl.multiple_of(c * width, width), width)],
            geno.at[c], geno_sem.at[c])

    def remote(src, dst, send, recv, there):
        return pltpu.make_async_remote_copy(
            src_ref=src, dst_ref=dst, send_sem=send, recv_sem=recv,
            device_id={"rows": there}, device_id_type=MESH)

    def whole_push(r, level, slot):
        return remote(whole.at[r, z], whole.at[r, slot], whole_send.at[r, level],
                      whole_recv.at[r, slot], at(level, i))

    def panel_push(r, level, j, slot):
        return remote(stage.at[r, at(level, j)], panels.at[r, at(level, slot)],
                      panel_send.at[r, at(level, j)], panel_recv.at[r, at(level, slot)], at(z, j))

    def term_push(r, level, j, slot):
        return remote(outgoing.at[r, at(level, j)], terms.at[r, at(level, slot)],
                      term_send.at[r, at(level, j)], term_recv.at[r, at(level, slot)], at(z, j))

    def part_push(r, level, slot):
        return remote(part_out.at[r, level], part_in.at[r, slot], part_send.at[r, level],
                      part_recv.at[r, slot], at(level, i))

    barrier = pltpu.get_barrier_semaphore()

    @pl.loop(1, group)
    def _(j):
        pl.semaphore_signal(barrier, inc=1, device_id={"rows": at(z, mate(j))}, device_id_type=MESH)

    @pl.loop(1, levels)
    def _(d):
        pl.semaphore_signal(barrier, inc=1, device_id={"rows": at(after(d), i)}, device_id_type=MESH)

    @pl.loop(0, levels)
    def _(d):
        for j in range(group):
            geno_copy(at(before(d), mate(j))).start()

    st[...] = st_in[...]
    for p in range(own // 2):
        pairs[p] = vt_in[:, p * two:(p + 1) * two]

    def local(b, s, k):
        return jnp.clip(cov_ref[b, s * per + k] - s * own, 0, own - 1)

    def select(level, b):
        def block(k):
            index = local(b, at(level, i), k)
            both = seen[lax.div(index, 2)]
            return jnp.where(lax.rem(index, 2) == 0, both[:, :tile], both[:, tile:])

        return jnp.concatenate([block(k) for k in range(per)], axis=1).astype(BF16)

    place = lax.broadcasted_iota(jnp.int32, (1, width), 1) // tile
    first = lax.broadcasted_iota(jnp.int32, (1, two), 1) < tile

    def listed(b, s):
        out = jnp.full((1, width), local(b, s, 0), jnp.int32)
        for k in range(1, per):
            out = jnp.where(place == k, local(b, s, k), out)
        return out

    count[...] = jnp.zeros_like(count)

    @pl.loop(0, n)
    def _(b):
        row = listed(b, me)
        for c in range(own):
            count[c:c + 1, :] += (row == c).astype(F32)

    pl.semaphore_wait(barrier, group + levels - 2)

    step = 0.5 * math.sqrt(rank) / (n * per * tile)
    for r in range(ROUNDS):
        whole[r, z] = pairs[...].astype(BF16)

        @pl.loop(1, levels)
        def _(d):
            whole_push(r, after(d), z).start()

        def hand_on(level):
            seen[...] = whole[r, level].astype(F32)
            for j in range(1, group):
                stage[r, at(level, mate(j))] = select(level, at(z, mate(j)))
                panel_push(r, level, mate(j), i).start()
            panels[r, at(level, i)] = select(level, me)

        def sample_terms(level, square):
            for j in range(group):
                s = at(level, mate(j))
                if j > 0:
                    panel_push(r, level, mate(j), mate(j)).wait_recv()
                if r == 0:
                    geno_copy(s).wait()
                panel = panels[r, s]
                acc[...] += nt(geno[s], panel)
                square = square + nt(panel, panel)
            return square

        hand_on(z)
        st_bf[...] = st[...].astype(BF16)
        acc[...] = jnp.zeros_like(acc)

        def sample_body(d, square):
            whole_push(r, before(d), before(d)).wait_recv()
            hand_on(before(d))
            return sample_terms(before(d - 1), square)

        square = lax.fori_loop(1, levels, sample_body, jnp.zeros((rank, rank), F32))
        square = sample_terms(before(levels - 1), square)
        now = st_bf[...]
        fit = sum(nn(part, now) for part in three_terms(square))
        fresh = (1.0 - DECAY) * st[...] + step * (acc[...].T - fit)
        st[...] = fresh
        now = fresh.astype(BF16)
        st_bf[...] = now

        gram = three_terms(nt(now, now))

        def snp_term(s):
            panel = panels[r, s]
            fit = sum(nn(part, panel) for part in gram)
            return (nn(st_bf[...], geno[s]) - fit).astype(BF16)

        def send_terms(level):
            for j in range(1, group):
                outgoing[r, at(level, mate(j))] = snp_term(at(level, mate(j)))
                term_push(r, level, mate(j), i).start()

        def fold(c):
            out = total[c, :, :two]
            for k in range(1, width // two):
                out = out + total[c, :, k * two:(k + 1) * two]
            return out + pltpu.roll(out, tile, 1)

        def add_up(level):
            owner = at(level, i)
            total[...] = jnp.zeros_like(total)
            for j in range(group):
                if j == 0:
                    value = snp_term(owner)
                else:
                    term_push(r, level, mate(j), mate(j)).wait_recv()
                    value = terms[r, at(level, mate(j))]
                row = listed(at(z, mate(j)), owner)
                wide = value.astype(F32)
                for c in range(own):
                    total[c] += jnp.where(row == c, wide, 0.0)
            return [jnp.where(first, fold(2 * p), fold(2 * p + 1)) for p in range(own // 2)]

        def send_part(level):
            for p, value in enumerate(add_up(level)):
                part_out[r, level, p] = value.astype(BF16)
            part_push(r, level, z).start()

        send_terms(after(1))

        @pl.loop(1, levels)
        def _(d):
            send_terms(after(d + 1))
            send_part(after(d))

        for p, value in enumerate(add_up(z)):
            grads[p] = value

        @pl.loop(1, levels)
        def _(d):
            part_push(r, before(d), before(d)).wait_recv()
            grads[...] += part_in[r, before(d)].astype(F32)

        def rate(c):
            observed = jnp.sum(count[c:c + 1, :], axis=1, keepdims=True) / tile
            return 0.5 * math.sqrt(rank) / (rows * observed)

        for p in range(own // 2):
            pairs[p] = (1.0 - DECAY) * pairs[p] + jnp.where(first, rate(2 * p), rate(2 * p + 1)) * grads[p]

    st_out[...] = st[...]
    for p in range(own // 2):
        vt_out[:, p * two:(p + 1) * two] = pairs[p]

    for r in range(ROUNDS):
        @pl.loop(1, levels)
        def _(d):
            whole_push(r, after(d), z).wait_send()
            part_push(r, after(d), z).wait_send()

        @pl.loop(0, levels)
        def _(level):
            for j in range(1, group):
                panel_push(r, level, mate(j), i).wait_send()
                term_push(r, level, mate(j), i).wait_send()


def on_device(genotypes, sample_factors, snp_factors, coverage):
    n = lax.axis_size("rows")
    rows, rank = sample_factors.shape
    covered = coverage.shape[1]
    tile = genotypes.shape[1] // covered
    per = covered // n
    own = snp_factors.shape[0] // tile
    width = per * tile
    group = math.gcd(n, 4)
    levels = n // group
    half = own // 2
    st, vt = pl.pallas_call(
        functools.partial(kernel, n, group, per, own, tile),
        out_shape=(
            jax.ShapeDtypeStruct((rank, rows), F32),
            jax.ShapeDtypeStruct((rank, own * tile), F32),
        ),
        in_specs=[
            pl.BlockSpec(memory_space=pltpu.SMEM),
            pl.BlockSpec(memory_space=pl.ANY),
            pl.BlockSpec(memory_space=pltpu.VMEM),
            pl.BlockSpec(memory_space=pltpu.VMEM),
        ],
        out_specs=(
            pl.BlockSpec(memory_space=pltpu.VMEM),
            pl.BlockSpec(memory_space=pltpu.VMEM),
        ),
        scratch_shapes=[
            pltpu.VMEM((n, rows, width), BF16),
            pltpu.VMEM((ROUNDS, n, rank, width), BF16),
            pltpu.VMEM((ROUNDS, n, rank, width), BF16),
            pltpu.VMEM((ROUNDS, n, rank, width), BF16),
            pltpu.VMEM((ROUNDS, n, rank, width), BF16),
            pltpu.VMEM((ROUNDS, levels, half, rank, 2 * tile), BF16),
            pltpu.VMEM((ROUNDS, levels, half, rank, 2 * tile), BF16),
            pltpu.VMEM((ROUNDS, levels, half, rank, 2 * tile), BF16),
            pltpu.VMEM((half, rank, 2 * tile), F32),
            pltpu.VMEM((half, rank, 2 * tile), F32),
            pltpu.VMEM((half, rank, 2 * tile), F32),
            pltpu.VMEM((rank, rows), F32),
            pltpu.VMEM((rank, rows), BF16),
            pltpu.VMEM((rows, rank), F32),
            pltpu.VMEM((own, rank, width), F32),
            pltpu.VMEM((own, width), F32),
            pltpu.SemaphoreType.DMA((n,)),
            pltpu.SemaphoreType.DMA((ROUNDS, n)),
            pltpu.SemaphoreType.DMA((ROUNDS, n)),
            pltpu.SemaphoreType.DMA((ROUNDS, n)),
            pltpu.SemaphoreType.DMA((ROUNDS, n)),
            pltpu.SemaphoreType.DMA((ROUNDS, levels)),
            pltpu.SemaphoreType.DMA((ROUNDS, levels)),
            pltpu.SemaphoreType.DMA((ROUNDS, levels)),
            pltpu.SemaphoreType.DMA((ROUNDS, levels)),
        ],
        compiler_params=pltpu.CompilerParams(
            collective_id=0, has_side_effects=True, vmem_limit_bytes=52 * 1024 * 1024
        ),
    )(coverage, genotypes, sample_factors.T, snp_factors.T)
    return st.T, vt.T


def solution(mesh):
    placed = P(("groups", "rows"), None)
    return jax.shard_map(
        on_device,
        mesh=mesh,
        in_specs=(placed, placed, placed, P("groups", None)),
        out_specs=(placed, placed),
        check_vma=False,
    )
```

time: 68.6 us -> 71 us (1.035)
  the two profiles are of different devices: /device:TPU:13 before, /device:TPU:0 now
where the time goes in v2:
time: 71 us; the launch traced here: 70.8 us
  Pallas kernels  66.3 us (93%)
  local copies, waits for them, and re-layouts  3.93 us (6%)
    pallas_call x1, Pallas kernels, on_device(): pl.pallas_call(functools.partial(kernel, n, group, per, own, tile), out_s...  66.3 us
    unnamed x8, local copies, waits for them, and re-layouts  3.93 us

profile of v2, /device:TPU:0, one launch (start us, length us, event | category | flops | bytes accessed | tf_op | source)
XLA Modules:
  0.0 70.8 jit_solution(12196007376806841261)
XLA Ops:
  0.6 0.0 copy-start
  0.6 0.9 %copy-done = f32[1024,64]{0,1:T(8,128)S(1)} copy-done((f32[1024,64]{0,1:T(8,128)S(1)}, f32[1024,64]{0,1:T(8,128)}, u32[]{:S(2)}) %copy-start) | copy-done | bytes 262168
  1.6 0.0 copy-start.1
  1.6 0.9 %copy-done.1 = f32[640,64]{0,1:T(8,128)S(1)} copy-done((f32[640,64]{0,1:T(8,128)S(1)}, f32[640,64]{0,1:T(8,128)}, u32[]{:S(2)}) %copy-start.1) | copy-done | bytes 163864
  2.5 0.0 copy-start.2
  2.5 0.7 copy-done.2
  3.2 66.3 %shard_map.59 = (f32[64,1024]{1,0:T(8,128)S(1)}, f32[64,640]{1,0:T(8,128)S(1)}) custom-call(s32[16,64]{1,0:T(8,128)S(1)} %copy-done.2, bf16[1024,4096]{1,0:T(8,128)(2,1)} %geno_hbm.1, f32[64,1024]{1,0:T(8,128)S(1)} %bitcast.4, f32[64,640]{1,0:T(8,128)S(1)} %bitcast.7), custom_call_target="tpu_custom_call" | custom-call | tf_op jit(solution)/shard_map/pallas_call | solution.py:267
  69.5 0.7 copy.8
  70.2 0.7 copy.9
Async XLA Ops:
  0.6 1.0 %copy-start = (f32[1024,64]{0,1:T(8,128)S(1)}, f32[1024,64]{0,1:T(8,128)}, u32[]{:S(2)}) copy-start(f32[1024,64]{0,1:T(8,128)} %param.5) | copy-start | bytes 786436
  1.6 0.9 %copy-start.1 = (f32[640,64]{0,1:T(8,128)S(1)}, f32[640,64]{0,1:T(8,128)}, u32[]{:S(2)}) copy-start(f32[640,64]{0,1:T(8,128)} %param.6) | copy-start | bytes 491524
  2.5 0.7 copy-start.2

commit v3 on v2

--- a/solution.py
+++ b/solution.py
@@ -33,7 +33,7 @@
 
 def kernel(n, group, per, own, tile, cov_ref, geno_hbm, st_in, vt_in, st_out, vt_out,
            geno, panels, stage, terms, outgoing, whole, part_out, part_in, pairs, seen, grads,
-           st, st_bf, acc, total, count,
+           st, st_bf, acc, square, total, count,
            geno_sem, panel_send, panel_recv, term_send, term_recv,
            whole_send, whole_recv, part_send, part_recv):
     me = lax.axis_index("rows")
@@ -66,9 +66,11 @@
             src_ref=src, dst_ref=dst, send_sem=send, recv_sem=recv,
             device_id={"rows": there}, device_id_type=MESH)
 
-    def whole_push(r, level, slot):
-        return remote(whole.at[r, z], whole.at[r, slot], whole_send.at[r, level],
-                      whole_recv.at[r, slot], at(level, i))
+    def hop(r, slot, way):
+        return remote(whole.at[r, slot], whole.at[r, slot], whole_send.at[r, way, slot],
+                      whole_recv.at[r, slot], at(z - 1 + 2 * way, i))
+
+    has_left, has_right = z > 0, z < levels - 1
 
     def panel_push(r, level, j, slot):
         return remote(stage.at[r, at(level, j)], panels.at[r, at(level, slot)],
@@ -135,9 +137,13 @@
     for r in range(ROUNDS):
         whole[r, z] = pairs[...].astype(BF16)
 
-        @pl.loop(1, levels)
-        def _(d):
-            whole_push(r, after(d), z).start()
+        @pl.when(has_right)
+        def _():
+            hop(r, z, 1).start()
+
+        @pl.when(has_left)
+        def _():
+            hop(r, z, 0).start()
 
         def hand_on(level):
             seen[...] = whole[r, level].astype(F32)
@@ -146,7 +152,7 @@
                 panel_push(r, level, mate(j), i).start()
             panels[r, at(level, i)] = select(level, me)
 
-        def sample_terms(level, square):
+        def sample_terms(level):
             for j in range(group):
                 s = at(level, mate(j))
                 if j > 0:
@@ -155,22 +161,50 @@
                     geno_copy(s).wait()
                 panel = panels[r, s]
                 acc[...] += nt(geno[s], panel)
-                square = square + nt(panel, panel)
-            return square
+                square[...] += nt(panel, panel)
 
         hand_on(z)
         st_bf[...] = st[...].astype(BF16)
         acc[...] = jnp.zeros_like(acc)
 
-        def sample_body(d, square):
-            whole_push(r, before(d), before(d)).wait_recv()
-            hand_on(before(d))
-            return sample_terms(before(d - 1), square)
-
-        square = lax.fori_loop(1, levels, sample_body, jnp.zeros((rank, rank), F32))
-        square = sample_terms(before(levels - 1), square)
+        square[...] = jnp.zeros_like(square)
+
+        @pl.loop(1, levels + 1)
+        def _(d):
+            @pl.when(z - d >= 0)
+            def _():
+                hop(r, z - d, 1).wait_recv()
+
+                @pl.when(has_right)
+                def _():
+                    hop(r, z - d, 1).start()
+
+            @pl.when(z + d < levels)
+            def _():
+                hop(r, z + d, 0).wait_recv()
+
+                @pl.when(has_left)
+                def _():
+                    hop(r, z + d, 0).start()
+
+            @pl.when(z - d >= 0)
+            def _():
+                hand_on(z - d)
+
+            @pl.when(z + d < levels)
+            def _():
+                hand_on(z + d)
+
+            @pl.when(z - d + 1 >= 0)
+            def _():
+                sample_terms(z - d + 1)
+
+            @pl.when((d > 1) & (z + d - 1 < levels))
+            def _():
+                sample_terms(z + d - 1)
+
         now = st_bf[...]
-        fit = sum(nn(part, now) for part in three_terms(square))
+        fit = sum(nn(part, now) for part in three_terms(square[...]))
         fresh = (1.0 - DECAY) * st[...] + step * (acc[...].T - fit)
         st[...] = fresh
         now = fresh.astype(BF16)
@@ -243,11 +277,18 @@
     for r in range(ROUNDS):
         @pl.loop(1, levels)
         def _(d):
-            whole_push(r, after(d), z).wait_send()
             part_push(r, after(d), z).wait_send()
 
         @pl.loop(0, levels)
         def _(level):
+            @pl.when(has_right & (level <= z))
+            def _():
+                hop(r, level, 1).wait_send()
+
+            @pl.when(has_left & (level >= z))
+            def _():
+                hop(r, level, 0).wait_send()
+
             for j in range(1, group):
                 panel_push(r, level, mate(j), i).wait_send()
                 term_push(r, level, mate(j), i).wait_send()
@@ -295,6 +336,7 @@
             pltpu.VMEM((rank, rows), F32),
             pltpu.VMEM((rank, rows), BF16),
             pltpu.VMEM((rows, rank), F32),
+            pltpu.VMEM((rank, rank), F32),
             pltpu.VMEM((own, rank, width), F32),
             pltpu.VMEM((own, width), F32),
             pltpu.SemaphoreType.DMA((n,)),
@@ -302,7 +344,7 @@
             pltpu.SemaphoreType.DMA((ROUNDS, n)),
             pltpu.SemaphoreType.DMA((ROUNDS, n)),
             pltpu.SemaphoreType.DMA((ROUNDS, n)),
-            pltpu.SemaphoreType.DMA((ROUNDS, levels)),
+            pltpu.SemaphoreType.DMA((ROUNDS, 2, levels)),
             pltpu.SemaphoreType.DMA((ROUNDS, levels)),
             pltpu.SemaphoreType.DMA((ROUNDS, levels)),
             pltpu.SemaphoreType.DMA((ROUNDS, levels)),

time: 71 us -> 67.2 us (0.946)
  Pallas kernels: 66.3 us -> 62.4 us
    pallas_call x1, Pallas kernels: 66.3 us -> 62.4 us  [on_device(): pl.pallas_call(functools.partial(kernel, n, group, per, own, tile), out_s...]
where the time goes in v3:
time: 67.2 us; the launch traced here: 67 us
  Pallas kernels  62.4 us (93%)
  local copies, waits for them, and re-layouts  3.93 us (6%)
    pallas_call x1, Pallas kernels, on_device(): pl.pallas_call(functools.partial(kernel, n, group, per, own, tile), out_s...  62.4 us
    unnamed x8, local copies, waits for them, and re-layouts  3.93 us

profile of v3, /device:TPU:0, one launch (start us, length us, event | category | flops | bytes accessed | tf_op | source)
XLA Modules:
  0.0 67.0 jit_solution(11017113833807202310)
XLA Ops:
  0.6 0.0 copy-start
  0.6 0.9 %copy-done = f32[1024,64]{0,1:T(8,128)S(1)} copy-done((f32[1024,64]{0,1:T(8,128)S(1)}, f32[1024,64]{0,1:T(8,128)}, u32[]{:S(2)}) %copy-start) | copy-done | bytes 262168
  1.6 0.0 copy-start.1
  1.6 0.9 %copy-done.1 = f32[640,64]{0,1:T(8,128)S(1)} copy-done((f32[640,64]{0,1:T(8,128)S(1)}, f32[640,64]{0,1:T(8,128)}, u32[]{:S(2)}) %copy-start.1) | copy-done | bytes 163864
  2.5 0.0 copy-start.2
  2.5 0.7 %copy-done.2 = s32[16,64]{1,0:T(8,128)S(1)} copy-done((s32[16,64]{1,0:T(8,128)S(1)}, s32[16,64]{1,0:T(8,128)}, u32[]{:S(2)}) %copy-start.2) | copy-done | bytes 4120
  3.2 62.4 %shard_map.59 = (f32[64,1024]{1,0:T(8,128)S(1)}, f32[64,640]{1,0:T(8,128)S(1)}) custom-call(s32[16,64]{1,0:T(8,128)S(1)} %copy-done.2, bf16[1024,4096]{1,0:T(8,128)(2,1)} %geno_hbm.1, f32[64,1024]{1,0:T(8,128)S(1)} %bitcast.4, f32[64,640]{1,0:T(8,128)S(1)} %bitcast.7), custom_call_target="tpu_custom_call" | custom-call | tf_op jit(solution)/shard_map/pallas_call | solution.py:308
  65.6 0.7 %copy.8 = f32[1024,64]{0,1:T(8,128)} copy(f32[1024,64]{0,1:T(8,128)S(1)} %bitcast.5) | data formatting | bytes 524288
  66.3 0.7 copy.9
Async XLA Ops:
  0.6 1.0 %copy-start = (f32[1024,64]{0,1:T(8,128)S(1)}, f32[1024,64]{0,1:T(8,128)}, u32[]{:S(2)}) copy-start(f32[1024,64]{0,1:T(8,128)} %param.5) | copy-start | bytes 786436
  1.6 0.9 %copy-start.1 = (f32[640,64]{0,1:T(8,128)S(1)}, f32[640,64]{0,1:T(8,128)}, u32[]{:S(2)}) copy-start(f32[640,64]{0,1:T(8,128)} %param.6) | copy-start | bytes 491524
  2.5 0.7 %copy-start.2 = (s32[16,64]{1,0:T(8,128)S(1)}, s32[16,64]{1,0:T(8,128)}, u32[]{:S(2)}) copy-start(s32[16,64]{1,0:T(8,128)} %cov_ref.1) | copy-start | bytes 12292

commit v4 on v3

--- a/solution.py
+++ b/solution.py
@@ -58,7 +58,7 @@
 
     def geno_copy(c):
         return pltpu.make_async_copy(
-            geno_hbm.at[:, pl.ds(pl.multiple_of(c * width, width), width)],
+            geno_hbm.at[:, pl.ds(pl.multiple_of(c * group * width, group * width), group * width)],
             geno.at[c], geno_sem.at[c])
 
     def remote(src, dst, send, recv, there):
@@ -96,8 +96,7 @@
 
     @pl.loop(0, levels)
     def _(d):
-        for j in range(group):
-            geno_copy(at(before(d), mate(j))).start()
+        geno_copy(before(d)).start()
 
     st[...] = st_in[...]
     for p in range(own // 2):
@@ -153,15 +152,13 @@
             panels[r, at(level, i)] = select(level, me)
 
         def sample_terms(level):
-            for j in range(group):
-                s = at(level, mate(j))
-                if j > 0:
-                    panel_push(r, level, mate(j), mate(j)).wait_recv()
-                if r == 0:
-                    geno_copy(s).wait()
-                panel = panels[r, s]
-                acc[...] += nt(geno[s], panel)
-                square[...] += nt(panel, panel)
+            for j in range(1, group):
+                panel_push(r, level, mate(j), mate(j)).wait_recv()
+            if r == 0:
+                geno_copy(level).wait()
+            panel = jnp.concatenate([panels[r, at(level, j)] for j in range(group)], axis=1)
+            acc[...] += nt(geno[level], panel)
+            square[...] += nt(panel, panel)
 
         hand_on(z)
         st_bf[...] = st[...].astype(BF16)
@@ -215,7 +212,9 @@
         def snp_term(s):
             panel = panels[r, s]
             fit = sum(nn(part, panel) for part in gram)
-            return (nn(st_bf[...], geno[s]) - fit).astype(BF16)
+            start = pl.multiple_of(lax.rem(s, group) * width, width)
+            seen_geno = geno[lax.div(s, group), :, pl.ds(start, width)]
+            return (nn(st_bf[...], seen_geno) - fit).astype(BF16)
 
         def send_terms(level):
             for j in range(1, group):
@@ -322,7 +321,7 @@
             pl.BlockSpec(memory_space=pltpu.VMEM),
         ),
         scratch_shapes=[
-            pltpu.VMEM((n, rows, width), BF16),
+            pltpu.VMEM((levels, rows, group * width), BF16),
             pltpu.VMEM((ROUNDS, n, rank, width), BF16),
             pltpu.VMEM((ROUNDS, n, rank, width), BF16),
             pltpu.VMEM((ROUNDS, n, rank, width), BF16),
@@ -339,7 +338,7 @@
             pltpu.VMEM((rank, rank), F32),
             pltpu.VMEM((own, rank, width), F32),
             pltpu.VMEM((own, width), F32),
-            pltpu.SemaphoreType.DMA((n,)),
+            pltpu.SemaphoreType.DMA((levels,)),
             pltpu.SemaphoreType.DMA((ROUNDS, n)),
             pltpu.SemaphoreType.DMA((ROUNDS, n)),
             pltpu.SemaphoreType.DMA((ROUNDS, n)),

time: 67.2 us -> 65.6 us (0.976)
  Pallas kernels: 62.4 us -> 60.8 us
    pallas_call x1, Pallas kernels: 62.4 us -> 60.8 us  [on_device(): pl.pallas_call(functools.partial(kernel, n, group, per, own, tile), out_s...]
where the time goes in v4:
time: 65.6 us; the launch traced here: 65.4 us
  Pallas kernels  60.8 us (93%)
  local copies, waits for them, and re-layouts  3.93 us (6%)
    pallas_call x1, Pallas kernels, on_device(): pl.pallas_call(functools.partial(kernel, n, group, per, own, tile), out_s...  60.8 us
    unnamed x8, local copies, waits for them, and re-layouts  3.93 us

profile of v4, /device:TPU:0, one launch (start us, length us, event | category | flops | bytes accessed | tf_op | source)
XLA Modules:
  0.0 65.4 jit_solution(10756876092610117243)
XLA Ops:
  0.6 0.0 copy-start
  0.6 0.9 %copy-done = f32[1024,64]{0,1:T(8,128)S(1)} copy-done((f32[1024,64]{0,1:T(8,128)S(1)}, f32[1024,64]{0,1:T(8,128)}, u32[]{:S(2)}) %copy-start) | copy-done | bytes 262168
  1.6 0.0 copy-start.1
  1.6 0.9 %copy-done.1 = f32[640,64]{0,1:T(8,128)S(1)} copy-done((f32[640,64]{0,1:T(8,128)S(1)}, f32[640,64]{0,1:T(8,128)}, u32[]{:S(2)}) %copy-start.1) | copy-done | bytes 163864
  2.5 0.0 copy-start.2
  2.5 0.7 %copy-done.2 = s32[16,64]{1,0:T(8,128)S(1)} copy-done((s32[16,64]{1,0:T(8,128)S(1)}, s32[16,64]{1,0:T(8,128)}, u32[]{:S(2)}) %copy-start.2) | copy-done | bytes 4120
  3.2 60.8 %shard_map.59 = (f32[64,1024]{1,0:T(8,128)S(1)}, f32[64,640]{1,0:T(8,128)S(1)}) custom-call(s32[16,64]{1,0:T(8,128)S(1)} %copy-done.2, bf16[1024,4096]{1,0:T(8,128)(2,1)} %geno_hbm.1, f32[64,1024]{1,0:T(8,128)S(1)} %bitcast.4, f32[64,640]{1,0:T(8,128)S(1)} %bitcast.7), custom_call_target="tpu_custom_call" | custom-call | tf_op jit(solution)/shard_map/pallas_call | solution.py:307
  64.0 0.7 %copy.8 = f32[1024,64]{0,1:T(8,128)} copy(f32[1024,64]{0,1:T(8,128)S(1)} %bitcast.5) | data formatting | bytes 524288
  64.7 0.7 %copy.9 = f32[640,64]{0,1:T(8,128)} copy(f32[640,64]{0,1:T(8,128)S(1)} %bitcast.6) | data formatting | bytes 327680
Async XLA Ops:
  0.6 1.0 %copy-start = (f32[1024,64]{0,1:T(8,128)S(1)}, f32[1024,64]{0,1:T(8,128)}, u32[]{:S(2)}) copy-start(f32[1024,64]{0,1:T(8,128)} %param.5) | copy-start | bytes 786436
  1.6 0.9 %copy-start.1 = (f32[640,64]{0,1:T(8,128)S(1)}, f32[640,64]{0,1:T(8,128)}, u32[]{:S(2)}) copy-start(f32[640,64]{0,1:T(8,128)} %param.6) | copy-start | bytes 491524
  2.5 0.7 %copy-start.2 = (s32[16,64]{1,0:T(8,128)S(1)}, s32[16,64]{1,0:T(8,128)}, u32[]{:S(2)}) copy-start(s32[16,64]{1,0:T(8,128)} %cov_ref.1) | copy-start | bytes 12292
